TPU v7x, 256 devices: a whole 4x4x8 slice. The times are simulated.
256 devices in a mesh: section: 2 (over core), ep: 32 (over x, z), tp: 4 (over y).
Axes of the slice: x: 4, y: 4, z: 8, core: 2. Of those that a mesh axis runs over, the one named last changes fastest.
Arguments:
- out_grad: bfloat16 [2, 4096, 7168], P('section', 'ep', 'tp'), may hold values from -6 to 6
- expert_ids: int32 [2, 4096, 8], P('section', 'ep'), may hold values from 0 to 31, all different within a row; in each aligned block of 128 rows (0 to 127, 128 to 255, ..., all dimensions but the last counted through in order) at most 40 rows name the same one
- gates: float32 [2, 4096, 8], P('section', 'ep'), may hold values from 0.05 to 0.6
- w_gate: bfloat16 [2, 32, 7168, 1024], P('section', 'ep', 'tp'), may hold values from -0.0625 to 0.0625
- w_up: bfloat16 [2, 32, 7168, 1024], P('section', 'ep', 'tp'), may hold values from -0.0625 to 0.0625
- w_down: bfloat16 [2, 32, 1024, 7168], P('section', 'ep', None, 'tp'), may hold values from -0.1875 to 0.1875
- gate_saved: bfloat16 [2, 32, 1024, 1280], P('section', 'ep', 'tp'), may hold values from -4 to 4
- up_saved: bfloat16 [2, 32, 1024, 1280], P('section', 'ep', 'tp'), may hold values from -4 to 4
Outputs:
- handed_grad: bfloat16 [2, 4096, 7168], P('section', 'ep', 'tp')
Inputs may be any that keep to these rules, and one draw needn't show every extreme that they name: `expert_ids`: each row names 8 different experts; within one section, the rows of one index of ep name any expert at most 40 times, a bound that some block reaches.
All inputs are finite; a program needn't handle non-finite values.
Results may differ from a plain program's by a relative error of at most 0.0057.
Values may be sent and summed in bfloat16 or wider, within the bound.
A program may use at most 128 MiB of HBM per device.

v0:
```python
import jax
import jax.numpy as jnp
from jax import lax
from jax.sharding import PartitionSpec as P


def from_partner(block, axis, stride):
    count = lax.axis_size(axis)
    route = []
    for low in range(count):
        high = low | 1 << stride
        if high != low and high < count:
            route += [(low, high), (high, low)]
    return lax.ppermute(block, axis, route)


def hidden_grads(hidden_sum, gate_part, up_part):
    pre = gate_part.astype(jnp.float32)
    upward = up_part.astype(jnp.float32)
    sigma = jax.nn.sigmoid(pre)
    up_grad = (hidden_sum * pre * sigma).astype(jnp.bfloat16)
    gate_grad = (hidden_sum * upward * sigma * (1.0 + pre * (1.0 - sigma))).astype(jnp.bfloat16)
    return (gate_grad, up_grad)


def shards(out_grad, expert_ids, gates, w_gate, w_up, w_down, gate_saved, up_saved):
    owners = lax.axis_size("ep")
    grad_rows = out_grad[0]
    routes = expert_ids[0]
    route_gates = gates[0]
    count_rows, fanout = routes.shape
    width = grad_rows.shape[1]
    slots_all = gate_saved.shape[-1]
    capacity = slots_all // owners
    token_of = jnp.arange(count_rows, dtype=jnp.int32)
    onehot = jnp.sum(
        (routes[:, :, None] == jnp.arange(owners, dtype=jnp.int32)).astype(jnp.int32),
        axis=1,
        dtype=jnp.int32,
    )
    before = jnp.cumsum(onehot, axis=0, dtype=jnp.int32) - onehot
    position = jnp.take_along_axis(before, routes, axis=1)
    slot = routes * capacity + position
    slot_token = (
        jnp.full((owners * capacity,), -1, jnp.int32)
        .at[slot.reshape(-1)]
        .set(jnp.repeat(token_of, fanout))
    )
    filled = slot_token >= 0
    send = jnp.where(
        filled[:, None], grad_rows[jnp.maximum(slot_token, 0)], jnp.zeros((), jnp.bfloat16)
    )
    send = send.reshape(owners, capacity, width)
    down_local = w_down[0, 0]
    gate_local = w_gate[0, 0]
    up_local = w_up[0, 0]
    contract = (((1,), (1,)), ((), ()))
    arrived = lax.all_to_all(send, "ep", split_axis=0, concat_axis=0, tiled=True).reshape(-1, width)
    terms = lax.dot_general(down_local, arrived, contract, preferred_element_type=jnp.float32)
    hidden_sum = lax.psum_scatter(terms, "tp", scatter_dimension=0, tiled=True)
    gate_grad, up_grad = hidden_grads(hidden_sum, gate_saved[0, 0], up_saved[0, 0])
    gate_full, up_full = (
        lax.all_gather(gate_grad, "tp", axis=0, tiled=True),
        lax.all_gather(up_grad, "tp", axis=0, tiled=True),
    )
    slot_grad = jnp.einsum("fs,df->sd", gate_full, gate_local, preferred_element_type=jnp.float32)
    slot_grad = slot_grad + jnp.einsum(
        "fs,df->sd", up_full, up_local, preferred_element_type=jnp.float32
    )
    slot_grad = slot_grad.astype(jnp.bfloat16).reshape(owners, capacity, width)
    returned = lax.all_to_all(slot_grad, "ep", split_axis=0, concat_axis=0, tiled=True).reshape(
        owners * capacity, width
    )
    total = jnp.zeros((count_rows, width), jnp.float32)
    for index in range(fanout):
        total = total + route_gates[:, index][:, None] * returned[slot[:, index]].astype(
            jnp.float32
        )
    handed = from_partner(total.astype(jnp.bfloat16), "section", 0)
    return handed[None]


def solution(mesh):
    return jax.shard_map(
        shards,
        mesh=mesh,
        in_specs=(
            P("section", "ep", "tp"),
            P("section", "ep", None),
            P("section", "ep", None),
            P("section", "ep", "tp", None),
            P("section", "ep", "tp", None),
            P("section", "ep", None, "tp"),
            P("section", "ep", "tp", None),
            P("section", "ep", "tp", None),
        ),
        out_specs=P("section", "ep", "tp"),
        check_vma=False,
    )
```

profile of v0, /device:TPU:1, one launch (start us, length us, event | category | flops | bytes accessed | tf_op | source)
XLA Modules:
  0.0 470.9 jit_solution(15922557636898809505)
XLA Ops:
  6.5 0.0 copy-start
  6.5 0.7 fusion.24
  7.3 0.8 copy.22
  8.1 0.7 convert_reduce_fusion
  8.8 0.1 copy.25
  8.9 0.1 copy.27
  9.0 0.1 reshape.212
  9.1 0.1 squeeze.15
  9.2 0.2 reduce_window_sum.11
  9.4 0.1 reshape.222
  9.5 7.1 %gather_fusion.9 = s32[1024]{0:T(1024)S(1)} fusion(s32[128,32]{1,0:T(8,128)S(1)} %sub.6, s32[1024]{0:T(1024)S(1)} %reshape.212), kind=kCustom, calls=%fused_computation.9 | custom fusion | bytes 16384 | tf_op jit(solution)/shard_map/jit(take_along_axis)/gather | solution.py:42
  16.6 4.3 scatter_custom_fusion
  20.9 0.1 broadcast_in_dim.46
  21.0 5.8 %gather_fusion = bf16[1280,1792]{1,0:T(8,128)(2,1)} fusion(bf16[128,1792]{1,0:T(8,128)(2,1)S(1)} %bitcast.59, s32[2048]{0:T(1024)S(1)} %pad_clamp_fusion), kind=kCustom, calls=%fused_computation | custom fusion | bytes 9180160 | tf_op jit(solution)/shard_map/gather | solution.py:51
  26.8 2.7 broadcast_select_fusion
  29.5 0.0 copy-start.4
  29.5 113.5 %all_to_all.10 = bf16[32,40,1792]{2,1,0:T(8,128)(2,1)S(1)} all-to-all(bf16[32,40,1792]{2,1,0:T(8,128)(2,1)S(1)} %broadcast_select_fusion), channel_id=1, replica_groups=mesh['section'=2,'ep'=32,'tp'=4] {'ep'}, dimensions={0} | all-to-all | bytes 9175040 | tf_op jit(solution)/shard_map/all_to_all | solution.py:58
  143.1 6.8 %convolution_bitcast_fusion = f32[1024,1280]{0,1:T(8,128)} fusion(bf16[1280,1792]{1,0:T(8,128)(2,1)S(1)} %bitcast.62, bf16[1,1,1024,1792]{3,2,1,0:T(8,128)(2,1)S(1)} %copy-done.4), kind=kOutput, calls=%fused_computation.13 | convolution fusion | flops 4697620480 | bytes 13500416 | tf_op jit(solution)/shard_map/dot_general | solution.py:59
  149.9 0.0 reduce-scatter.2.cloned.1.call-update
  149.9 0.0 all-gather.3.cloned.1.call-start
  150.0 1.0 copy-done.1
  151.0 0.2 copy.29
  151.2 0.2 copy.28
  151.5 56.5 %reduce-scatter.2.cloned.1.call-done = f32[256,1280]{0,1:T(8,128)} async-done(((f32[1024,1280]{0,1:T(8,128)}), f32[256,1280]{0,1:T(8,128)}) %reduce-scatter.2.cloned.1.call-update) | async-done | bytes 1310736 | tf_op jit(solution)/shard_map/reduce_scatter | solution.py:60
  208.0 3.1 fusion.11
  211.0 0.0 all-gather.3.cloned.1.call-update
  211.1 0.2 all-gather.5.cloned.1.call-start
  211.3 0.5 all-gather.5.cloned.1.call-update
  211.8 39.7 %all-gather.3.cloned.1.call-done = bf16[1024,1280]{0,1:T(8,128)(2,1)} async-done(((bf16[256,1280]{0,1:T(8,128)(2,1)}), bf16[1024,1280]{0,1:T(8,128)(2,1)}) %all-gather.3.cloned.1.call-update) | async-done | bytes 2621456 | tf_op jit(solution)/shard_map/all_gather | solution.py:63
  251.5 11.3 %fusion.1 = f32[1280,1792]{1,0:T(8,128)} fusion(bf16[1024,1280]{0,1:T(8,128)(2,1)} %all-gather.3.cloned.1.call-done, bf16[1,1,1792,1024]{3,2,1,0:T(8,128)(2,1)} %param.11), kind=kOutput, calls=%fused_computation.15 | convolution fusion | flops 4697620480 | bytes 15466496 | tf_op jit(solution)/shard_map/fs,df->sd/dot_general | solution.py:66
  262.8 32.9 %all-gather.5.cloned.1.call-done = bf16[1024,1280]{0,1:T(8,128)(2,1)} async-done(((bf16[256,1280]{0,1:T(8,128)(2,1)}), bf16[1024,1280]{0,1:T(8,128)(2,1)}) %all-gather.5.cloned.1.call-update) | async-done | bytes 2621456 | tf_op jit(solution)/shard_map/all_gather | solution.py:64
  295.7 12.6 %add_convert_fusion = bf16[1280,1792]{1,0:T(8,128)(2,1)} fusion(f32[1280,1792]{1,0:T(8,128)} %fusion.1, bf16[1024,1280]{0,1:T(8,128)(2,1)} %all-gather.5.cloned.1.call-done, bf16[1,1,1792,1024]{3,2,1,0:T(8,128)(2,1)} %param.12), kind=kOutput, calls=%fused_computation.11 | convolution fusion | flops 4702208000 | bytes 20054016 | tf_op jit(solution)/shard_map/fs,df->sd/dot_general | solution.py:67
  308.3 10.0 %all-to-all-start.1 = ((bf16[32,40,1792]{2,1,0:T(8,128)(2,1)}), bf16[32,40,1792]{2,1,0:T(8,128)(2,1)}, u32[]{:S(2)}, u32[]{:S(2)}) async-start(bf16[32,40,1792]{2,1,0:T(8,128)(2,1)} %bitcast.61), calls=%async_computation.2 | async-start | bytes 9175040 | tf_op jit(solution)/shard_map/all_to_all | solution.py:71
  318.3 0.1 reshape.215
  318.5 0.4 fusion.13
  318.9 104.0 %all-to-all-done.1 = bf16[32,40,1792]{2,1,0:T(8,128)(2,1)} async-done(((bf16[32,40,1792]{2,1,0:T(8,128)(2,1)}), bf16[32,40,1792]{2,1,0:T(8,128)(2,1)}, u32[]{:S(2)}, u32[]{:S(2)}) %all-to-all-start.1) | async-done | bytes 4587552 | tf_op jit(solution)/shard_map/all_to_all | solution.py:71
  422.9 4.2 gather_fusion.8
  427.2 4.2 gather_fusion.7
  431.4 4.2 gather_fusion.6
  435.6 4.2 gather_fusion.5
  439.8 4.2 gather_fusion.4
  444.1 4.2 gather_fusion.3
  448.3 5.0 %gather_fusion.2 = bf16[128,1792]{1,0:T(8,128)(2,1)} fusion(bf16[1280,1792]{1,0:T(8,128)(2,1)} %bitcast.18, s32[1024]{0:T(1024)S(1)} %get-tuple-element.29), kind=kCustom, calls=%fused_computation.2 | custom fusion | bytes 918016 | tf_op jit(solution)/shard_map/gather | solution.py:76
  453.3 5.0 %gather_fusion.1 = bf16[128,1792]{1,0:T(8,128)(2,1)} fusion(bf16[1280,1792]{1,0:T(8,128)(2,1)} %bitcast.18, s32[1024]{0:T(1024)S(1)} %get-tuple-element.30), kind=kCustom, calls=%fused_computation.1 | custom fusion | bytes 918016 | tf_op jit(solution)/shard_map/gather | solution.py:76
  458.3 1.9 add_convert_fusion.1
  460.2 1.9 collective-permute-start
  462.2 1.4 collective-permute-done
  463.6 0.8 copy.32
  (20 shorter events, 0.1 us)
Async XLA Ops:
  6.5 14.5 %copy-start = (bf16[1,128,1792]{2,1,0:T(8,128)(2,1)S(1)}, bf16[1,128,1792]{2,1,0:T(8,128)(2,1)}, u32[]{:S(2)}) copy-start(bf16[1,128,1792]{2,1,0:T(8,128)(2,1)} %param.8) | copy-start | bytes 1376260
  6.5 201.4 %reduce-scatter.2.cloned.1.call-start = ((), (), s32[]{:S(2)}) async-start(), calls=%async_computation.3 | async-start | bytes 6553600 | tf_op jit(solution)/shard_map/reduce_scatter | solution.py:60
  29.5 113.5 %copy-start.4 = (bf16[1,1,1024,1792]{3,2,1,0:T(8,128)(2,1)S(1)}, bf16[1,1,1024,1792]{3,2,1,0:T(8,128)(2,1)}, u32[]{:S(2)}) copy-start(bf16[1,1,1024,1792]{3,2,1,0:T(8,128)(2,1)} %param.13) | copy-start | bytes 11010052
  149.9 1.1 copy-start.1
  149.9 1.3 copy-start.2
  149.9 101.5 %all-gather.3.cloned.1.call-start = ((), (), s32[]{:S(2)}) async-start(), calls=%async_computation.4 | async-start | bytes 3276800 | tf_op jit(solution)/shard_map/all_gather | solution.py:63
  211.1 84.6 %all-gather.5.cloned.1.call-start = ((), (), s32[]{:S(2)}) async-start(), calls=%async_computation.5 | async-start | bytes 3276800 | tf_op jit(solution)/shard_map/all_gather | solution.py:64
  308.3 10.6 %copy-start.3 = (f32[1,128,8]{1,2,0:T(8,128)S(1)}, f32[1,128,8]{1,2,0:T(8,128)}, u32[]{:S(2)}) copy-start(f32[1,128,8]{1,2,0:T(8,128)} %param.10) | copy-start | bytes 12292
  308.3 114.6 %all-to-all-start.1 = ((bf16[32,40,1792]{2,1,0:T(8,128)(2,1)}), bf16[32,40,1792]{2,1,0:T(8,128)(2,1)}, u32[]{:S(2)}, u32[]{:S(2)}) async-start(bf16[32,40,1792]{2,1,0:T(8,128)(2,1)} %bitcast.61), calls=%async_computation.2 | async-start | bytes 9175040 | tf_op jit(solution)/shard_map/all_to_all | solution.py:71
  460.2 3.4 collective-permute-start
Sparse Core Ops, SparseCore 0:
  150.0 57.9 reduce-scatter.1
  211.2 40.2 all-gather.2
  253.3 42.3 all-gather.4
where the time goes:
time: 472 us; the launch traced here: 471 us
  waiting for transfers between devices  235 us (50%)
  blocking collectives  114 us (24%)
  local copies, waits for them, and re-layouts  56.2 us (12%)
  matrix products  30.7 us (7%)
  between operations  13.3 us (3%)
  starting transfers between devices  12.2 us (3%)
  other arithmetic  9.76 us (2%)
    all_to_all x1, blocking collectives, shards(): lax.all_to_all(send, 'ep', split_axis=0, concat_axis=0, tiled=True)  114 us
    all_to_all x1, waiting for transfers between devices, shards(): lax.all_to_all(slot_grad, 'ep', split_axis=0, concat_axis=0, tiled=True)  104 us
    reduce_scatter x1, waiting for transfers between devices, shards(): hidden_sum = lax.psum_scatter(terms, 'tp', scatter_dimension=0, tiled=True)  56.5 us
    all_gather x1, waiting for transfers between devices, shards(): lax.all_gather(gate_grad, 'tp', axis=0, tiled=True)  39.7 us
    gather x8, local copies, waits for them, and re-layouts, shards(): returned[slot[:, index]].astype(jnp.float32)  35.3 us
    all_gather x1, waiting for transfers between devices, shards(): lax.all_gather(up_grad, 'tp', axis=0, tiled=True)  32.9 us
    dot_general x1, matrix products, shards(): jnp.einsum('fs,df->sd', up_full, up_local, preferred_element_type=jnp.flo...  12.6 us
    dot_general x1, matrix products, shards(): jnp.einsum('fs,df->sd', gate_full, gate_local, preferred_element_type=jnp...  11.3 us
  transfers between devices with their start and end apart: 5, of which 5 were waited for; matrix products, arithmetic and copies ran while one was open for 3% of the time, Pallas kernels for 0%

commit v1 on v0

v1 whole, which is shorter than its diff:
```python
import jax
import jax.numpy as jnp
from jax import lax
from jax.experimental import pallas as pl
from jax.experimental.pallas import tpu as pltpu
from jax.sharding import PartitionSpec as P

MESH = pl.DeviceIdType.MESH
BF = jnp.bfloat16
F32 = jnp.float32
NX, NZ, NY = 4, 8, 4
TOK, W, FFL, CAP = 128, 1792, 256, 40
PAIR = 2 * CAP
CH = NX * PAIR
SLOTS = NX * NZ * CAP
PAIRS = ((0, 1), (-1, 2), (-2, 3), (-3, 4))
WHERE = {j: (c, h) for c, pair in enumerate(PAIRS) for h, j in enumerate(pair)}
NT = W // 256
WIRE = BF


def kernel(tokens, meta, wg, wu, wd, gsv, usv, out,
           tok, mt, sel, ghi, glo, xs, rows, hacc, part, hrecv, gu, ret, C, inp, inm, fin,
           gT, uT, gv, uv, wgv, wuv, wdv,
           agp_s, agp_r, agm_s, agm_r, mp_s, mp_r, mm_s, mm_r,
           xd_s, xd_r, yr_s, yr_r, yg_s, yg_r, xr_s, xr_r,
           rp_s, rp_r, rm_s, rm_r, f_s, f_r, loc):
    s = lax.axis_index("section")
    e = lax.axis_index("ep")
    y = lax.axis_index("tp")
    x = e // NZ
    z = lax.rem(e, NZ)

    def zdev(d):
        return (s, x * NZ + lax.rem(z + d + NZ, NZ), y)

    def xdev(o):
        return (s, lax.rem(x + o, NX) * NZ + z, y)

    def ydev(o):
        return (s, e, lax.rem(y + o, NY))

    partner = (1 - s, e, y)

    def remote(src, dst, ss, rs, dev):
        return pltpu.make_async_remote_copy(
            src_ref=src, dst_ref=dst, send_sem=ss, recv_sem=rs, device_id=dev, device_id_type=MESH)

    own_tok = pltpu.make_async_copy(tokens, tok.at[0, pl.ds(0, TOK)], loc.at[0])
    own_meta = pltpu.make_async_copy(meta, mt.at[0], loc.at[1])
    gcopy = pltpu.make_async_copy(gsv, gv, loc.at[2])
    ucopy = pltpu.make_async_copy(usv, uv, loc.at[3])
    dcopy = pltpu.make_async_copy(wd, wdv, loc.at[4])
    wgcopy = pltpu.make_async_copy(wg, wgv, loc.at[5])
    wucopy = pltpu.make_async_copy(wu, wuv, loc.at[6])
    for c in (own_tok, own_meta, gcopy, ucopy, dcopy, wgcopy, wucopy):
        c.start()

    barrier = pltpu.get_barrier_semaphore()
    peers = [zdev(1), zdev(-1)] + [xdev(o) for o in (1, 2, 3)] + [ydev(o) for o in (1, 2, 3)] + [partner]
    for dev in peers:
        pl.semaphore_signal(barrier, inc=1, device_id=dev, device_id_type=MESH)
    pl.semaphore_wait(barrier, len(peers))

    sends = []
    held = {}

    def begin(key, copy):
        copy.start()
        held[key] = copy
        sends.append(key)

    def arrived(key):
        held[key].wait_recv()

    def left(key):
        held[key].wait_send()
        sends.remove(key)

    def block(j, lo=0, n=TOK):
        c, h = WHERE[j]
        return tok.at[c, pl.ds(h * TOK + lo, n)]

    def metaof(j):
        c, h = WHERE[j]
        return mt.at[2 * c + h]

    half = TOK // 2

    def ag_send(d):
        k = d - 1
        if d < 4:
            begin(("ap", d), remote(block(k), block(d), agp_s.at[k], agp_r.at[k], zdev(-1)))
            begin(("am", d), remote(block(-k), block(-d), agm_s.at[k], agm_r.at[k], zdev(1)))
            begin(("mp", d), remote(metaof(k), metaof(d), mp_s.at[k], mp_r.at[k], zdev(-1)))
            begin(("mm", d), remote(metaof(-k), metaof(-d), mm_s.at[k], mm_r.at[k], zdev(1)))
        else:
            begin(("ap", d), remote(block(k, 0, half), block(4, 0, half), agp_s.at[k], agp_r.at[k], zdev(-1)))
            begin(("am", d), remote(block(-k, half, half), block(4, half, half), agm_s.at[k], agm_r.at[k], zdev(1)))
            begin(("mp", d), remote(metaof(k), metaof(4), mp_s.at[k], mp_r.at[k], zdev(-1)))

    def ag_wait(d):
        arrived(("mp", d))
        if d < 4:
            arrived(("mm", d))
        arrived(("ap", d))
        arrived(("am", d))

    def columns(n):
        return pl.ds(pl.multiple_of(n * 256, 256), 256)

    def select(c):
        t0 = lax.broadcasted_iota(jnp.int32, (TOK, TOK), 0)
        t1 = lax.broadcasted_iota(jnp.int32, (TOK, TOK), 1)
        earlier = (t0 < t1).astype(F32).astype(BF)
        rr = lax.broadcasted_iota(jnp.int32, (PAIR, 2 * TOK), 0)
        cc = lax.broadcasted_iota(jnp.int32, (PAIR, 2 * TOK), 1)
        same = (rr >= CAP) == (cc >= TOK)
        slot = jnp.where(rr >= CAP, rr - CAP, rr).astype(F32)
        r8 = lax.broadcasted_iota(jnp.int32, (8, TOK), 0)
        named, place, gate = [], [], []
        for h in range(2):
            ids = mt[2 * c + h, 0:8, :]
            gts = mt[2 * c + h, 8:16, :]
            m8 = jnp.zeros((8, TOK), F32)
            gs = []
            for o in range(NX):
                want = (lax.rem(x + o, NX) * NZ + z).astype(F32)
                hit = ids == want
                m = jnp.sum(hit.astype(F32), axis=0, keepdims=True)
                gs.append(jnp.sum(jnp.where(hit, gts, 0.0), axis=0, keepdims=True))
                m8 = jnp.where(r8 == o, m, m8)
            pos = jnp.dot(m8.astype(BF), earlier, preferred_element_type=F32)
            pos = jnp.where(m8 > 0.5, pos, -1.0)
            place.append(pos)
            gate.append(gs)
        for o in range(NX):
            pos2 = jnp.concatenate([place[0][o:o + 1], place[1][o:o + 1]], axis=1)
            g2 = jnp.concatenate([gate[0][o], gate[1][o]], axis=1)
            g_hi = g2.astype(BF).astype(F32)
            g_lo = g2 - g_hi
            hit = jnp.logical_and(slot == pos2, same)
            at = pl.ds(o * PAIR, PAIR)
            sel[c, at, :] = jnp.where(hit, 1.0, 0.0).astype(BF)
            ghi[c, at, :] = jnp.where(hit, g_hi, 0.0).astype(BF)
            glo[c, at, :] = jnp.where(hit, g_lo, 0.0).astype(BF)

        @pl.loop(0, NT)
        def _(n):
            got = jnp.dot(sel[c], tok[c, :, columns(n)], preferred_element_type=F32).astype(BF)
            rows[c, pl.ds(0, PAIR), columns(n)] = got[0:PAIR]
            xs[c, pl.ds(PAIR, 3 * PAIR), columns(n)] = got[PAIR:]

        for o in (2, 1, 3):
            begin(("xd", c, o), remote(xs.at[c, pl.ds(o * PAIR, PAIR)], rows.at[c, pl.ds((NX - o) * PAIR, PAIR)],
                                       xd_s.at[c, o - 1], xd_r.at[c, o - 1], xdev(o)))

    def first(c):
        for o in (1, 3, 2):
            arrived(("xd", c, o))
        for o in (1, 2, 3, 0):
            q = lax.rem(y + o, NY)
            acc = lax.dot_general(rows[c], wdv[columns(q), :], (((1,), (1,)), ((), ())), preferred_element_type=F32)
            if o:
                part[c, o - 1] = acc.astype(WIRE)
                begin(("yr", c, o), remote(part.at[c, o - 1], hrecv.at[c, o - 1], yr_s.at[c, o - 1], yr_r.at[c, o - 1], ydev(o)))
            else:
                hacc[c] = acc

    def grads(c):
        for o in (1, 2, 3):
            arrived(("yr", c, o))
        j1, j2 = PAIRS[c]
        for o in range(NX):
            at = pl.ds(o * PAIR, PAIR)
            h = hacc[c, at, :]
            for k in range(3):
                h = h + hrecv[c, k, at, :].astype(F32)
            base = lax.rem(x + o, NX) * NZ
            b1 = pl.ds(pl.multiple_of((base + lax.rem(z + j1 + NZ, NZ)) * CAP, 8), CAP)
            b2 = pl.ds(pl.multiple_of((base + lax.rem(z + j2 + NZ, NZ)) * CAP, 8), CAP)
            a = jnp.concatenate([gT[b1, :], gT[b2, :]], axis=0)
            u = jnp.concatenate([uT[b1, :], uT[b2, :]], axis=0)
            sigma = 1.0 / (1.0 + jnp.exp(-a))
            gu[c, y, 0, at, :] = (h * u * sigma * (1.0 + a * (1.0 - sigma))).astype(BF)
            gu[c, y, 1, at, :] = (h * a * sigma).astype(BF)
        for o in (2, 1, 3):
            begin(("yg", c, o), remote(gu.at[c, y], gu.at[c, y], yg_s.at[c, o - 1], yg_r.at[c, o - 1], ydev(o)))

    def second(c):
        for o in (1, 2, 3):
            left(("xd", c, o))
        for o in (1, 3, 2):
            src = lax.rem(y + NY - o, NY)
            remote(gu.at[c, src], gu.at[c, src], yg_s.at[c, o - 1], yg_r.at[c, o - 1], ydev(o)).wait_recv()

        @pl.loop(0, NT)
        def _(n):
            acc = jnp.zeros((CH, 256), F32)
            for q in range(NY):
                for i, w in ((0, wgv), (1, wuv)):
                    acc = acc + lax.dot_general(gu[c, q, i], w[columns(n), q * 256:(q + 1) * 256], (((1,), (1,)), ((), ())), preferred_element_type=F32)
            acc = acc.astype(BF)
            ret[c, pl.ds(0, PAIR), columns(n)] = acc[0:PAIR]
            xs[c, pl.ds(PAIR, 3 * PAIR), columns(n)] = acc[PAIR:]

    def give(c):
        for o in (2, 1, 3):
            begin(("xr", c, o), remote(xs.at[c, pl.ds(o * PAIR, PAIR)], ret.at[c, pl.ds((NX - o) * PAIR, PAIR)],
                                       xr_s.at[c, o - 1], xr_r.at[c, o - 1], xdev(o)))

    def combine(c):
        for o in (1, 3, 2):
            arrived(("xr", c, o))

        @pl.loop(0, NT)
        def _(n):
            r = ret[c, :, columns(n)]
            dims = (((0,), (0,)), ((), ()))
            C[c, :, columns(n)] = (lax.dot_general(ghi[c], r, dims, preferred_element_type=F32)
                                   + lax.dot_general(glo[c], r, dims, preferred_element_type=F32))

    def csum(j, lo, n, extra):
        c, h = WHERE[j]
        base = h * TOK + lo
        value = C[c, pl.ds(base, n), :]
        for r in extra:
            value = value + r.astype(F32)
        return value

    def chain(sign, j):
        inbox = inp if sign > 0 else inm
        ss, rs = (rp_s, rp_r) if sign > 0 else (rm_s, rm_r)
        name = "rp" if sign > 0 else "rm"
        dev = zdev(sign)
        lo = 0 if sign > 0 else half
        if j == 4:
            block(4, lo, half)[...] = csum(4, lo, half, ()).astype(BF)
            begin((name, j), remote(block(4, lo, half), inbox.at[3, pl.ds(lo, half)], ss.at[3], rs.at[3], dev))
            return
        arrived((name, j + 1))
        if j == 3:
            other = half - lo
            block(sign * j, lo, half)[...] = csum(sign * j, lo, half, (inbox[j, pl.ds(lo, half), :],)).astype(BF)
            block(sign * j, other, half)[...] = csum(sign * j, other, half, ()).astype(BF)
        else:
            block(sign * j)[...] = csum(sign * j, 0, TOK, (inbox[j],)).astype(BF)
        begin((name, j), remote(block(sign * j), inbox.at[j - 1], ss.at[j - 1], rs.at[j - 1], dev))

    own_tok.wait()
    own_meta.wait()
    ag_send(1)

    gcopy.wait()
    ucopy.wait()

    @pl.loop(0, SLOTS // 256)
    def _(i):
        gT[columns(i), :] = gv[:, columns(i)].astype(F32).T
        uT[columns(i), :] = uv[:, columns(i)].astype(F32).T

    ag_wait(1)
    ag_send(2)
    select(0)
    ag_wait(2)
    ag_send(3)
    select(1)
    dcopy.wait()
    first(0)
    ag_wait(3)
    ag_send(4)
    grads(0)
    ag_wait(4)
    select(3)
    select(2)
    for d in (1, 2, 3):
        for n in ("ap", "am", "mp", "mm"):
            left((n, d))
    for n in ("ap", "am", "mp"):
        left((n, 4))
    first(1)
    wgcopy.wait()
    wucopy.wait()
    second(0)
    grads(1)
    first(3)
    grads(3)
    second(1)
    first(2)
    give(0)
    give(1)
    grads(2)
    second(3)
    give(3)
    second(2)
    give(2)
    combine(0)
    combine(1)
    combine(3)
    chain(1, 4)
    chain(-1, 4)
    chain(-1, 3)
    combine(2)
    chain(1, 3)
    chain(-1, 2)
    chain(1, 2)
    chain(-1, 1)
    chain(1, 1)
    arrived(("rm", 1))
    arrived(("rp", 1))
    fin[...] = csum(0, 0, TOK, (inp[0], inm[0])).astype(BF)
    begin(("f",), remote(fin, out, f_s, f_r, partner))
    arrived(("f",))
    for key in list(sends):
        left(key)


def shards(out_grad, expert_ids, gates, w_gate, w_up, w_down, gate_saved, up_saved):
    meta = jnp.concatenate([expert_ids[0].T.astype(F32), gates[0].T], axis=0)
    dma = pltpu.SemaphoreType.DMA
    done = pl.pallas_call(
        kernel,
        out_shape=jax.ShapeDtypeStruct((TOK, W), BF),
        in_specs=[pl.BlockSpec(memory_space=pl.ANY)] * 7,
        out_specs=pl.BlockSpec(memory_space=pl.ANY),
        scratch_shapes=[
            pltpu.VMEM((4, 2 * TOK, W), BF),
            pltpu.VMEM((8, 16, TOK), F32),
            pltpu.VMEM((4, CH, 2 * TOK), BF),
            pltpu.VMEM((4, CH, 2 * TOK), BF),
            pltpu.VMEM((4, CH, 2 * TOK), BF),
            pltpu.VMEM((4, CH, W), BF),
            pltpu.VMEM((4, CH, W), BF),
            pltpu.VMEM((4, CH, FFL), F32),
            pltpu.VMEM((4, 3, CH, FFL), WIRE),
            pltpu.VMEM((4, 3, CH, FFL), WIRE),
            pltpu.VMEM((4, NY, 2, CH, FFL), BF),
            pltpu.VMEM((4, CH, W), BF),
            pltpu.VMEM((4, 2 * TOK, W), F32),
            pltpu.VMEM((4, TOK, W), BF),
            pltpu.VMEM((4, TOK, W), BF),
            pltpu.VMEM((TOK, W), BF),
            pltpu.VMEM((SLOTS, FFL), F32),
            pltpu.VMEM((SLOTS, FFL), F32),
            pltpu.VMEM((FFL, SLOTS), BF),
            pltpu.VMEM((FFL, SLOTS), BF),
            pltpu.VMEM((W, 1024), BF),
            pltpu.VMEM((W, 1024), BF),
            pltpu.VMEM((1024, W), BF),
        ] + [dma((4,))] * 8 + [dma((4, 3))] * 8 + [dma((4,))] * 4 + [dma, dma, dma((7,))],
        compiler_params=pltpu.CompilerParams(
            collective_id=0, has_side_effects=True, vmem_limit_bytes=63 * 2**20),
        cost_estimate=pl.CostEstimate(flops=16 * 10**9, bytes_accessed=14 * 10**6, transcendentals=3 * 10**5),
        name="expert_grad",
    )(out_grad[0], meta, w_gate[0, 0], w_up[0, 0], w_down[0, 0], gate_saved[0, 0], up_saved[0, 0])
    return done[None]


def solution(mesh):
    return jax.shard_map(
        shards,
        mesh=mesh,
        in_specs=(
            P("section", "ep", "tp"),
            P("section", "ep", None),
            P("section", "ep", None),
            P("section", "ep", "tp", None),
            P("section", "ep", "tp", None),
            P("section", "ep", None, "tp"),
            P("section", "ep", "tp", None),
            P("section", "ep", "tp", None),
        ),
        out_specs=P("section", "ep", "tp"),
        check_vma=False,
    )
```

time: 472 us -> 193 us (0.41)
  waiting for transfers between devices: 235 us -> 0 us
  Pallas kernels: 0 us -> 187 us
  blocking collectives: 114 us -> 0 us
  local copies, waits for them, and re-layouts: 56.2 us -> 1.82 us
  matrix products: 30.7 us -> 0 us
  between operations: 13.3 us -> 0.01 us
  starting transfers between devices: 12.2 us -> 0 us
  other arithmetic: 9.76 us -> 1.97 us
    pallas_call x0 -> x1, Pallas kernels: none -> 187 us  [shards(): pl.pallas_call(kernel, out_shape=jax.ShapeDtypeStruct((TOK, W), BF), in_s...]
    all_to_all x1 -> x0, blocking collectives: 114 us -> none  [shards(): lax.all_to_all(send, 'ep', split_axis=0, concat_axis=0, tiled=True)]
    all_to_all x1 -> x0, waiting for transfers between devices: 104 us -> none  [shards(): lax.all_to_all(slot_grad, 'ep', split_axis=0, concat_axis=0, tiled=True)]
    all_gather x2 -> x0, waiting for transfers between devices: 72.6 us -> none  [the longest x1 39.7 us: shards(): lax.all_gather(gate_grad, 'tp', axis=0, tiled=True)]
    reduce_scatter x1 -> x0, waiting for transfers between devices: 56.5 us -> none  [shards(): hidden_sum = lax.psum_scatter(terms, 'tp', scatter_dimension=0, tiled=True)]
    gather x13 -> x0, local copies, waits for them, and re-layouts: 48.5 us -> none  [the longest x8 35.3 us: shards(): returned[slot[:, index]].astype(jnp.float32)]
    dot_general x3 -> x0, matrix products: 30.7 us -> none  [the longest x1 12.6 us: shards(): jnp.einsum('fs,df->sd', up_full, up_local, preferred_element_type=jnp.flo...]
    all_to_all x1 -> x0, starting transfers between devices: 10 us -> none  [shards(): lax.all_to_all(slot_grad, 'ep', split_axis=0, concat_axis=0, tiled=True)]
  transfers between devices with their start and end apart: 5 -> 0, of which waited for: 5 -> 0; matrix products, arithmetic and copies ran while one was open for 3% -> 0% of each run, Pallas kernels for 0% -> 0%
where the time goes in v1:
time: 193 us; the launch traced here: 191 us
  Pallas kernels  187 us (97%)
  other arithmetic  1.97 us (1%)
    pallas_call x1, Pallas kernels, shards(): pl.pallas_call(kernel, out_shape=jax.ShapeDtypeStruct((TOK, W), BF), in_s...  187 us

profile of v1, /device:TPU:1, one launch (start us, length us, event | category | flops | bytes accessed | tf_op | source)
XLA Modules:
  0.0 191.3 jit_solution(6826333103978443858)
XLA Ops:
  0.0 0.7 convert_bitcast_fusion
  0.7 1.3 pad_maximum_fusion.meta
  2.0 187.5 %expert_grad.1 = bf16[128,1792]{1,0:T(8,128)(2,1)} custom-call(bf16[128,1792]{1,0:T(8,128)(2,1)} %bitcast.21, f32[16,128]{1,0:T(8,128)} %pad_maximum_fusion.meta, bf16[1792,1024]{1,0:T(8,128)(2,1)} %bitcast.16, bf16[1792,1024]{1,0:T(8,128)(2,1)} %bitcast.17, bf16[1024,1792]{1,0:T(8,128)(2,1)} %bitcast.18, bf16[256,1280]{1,0:T(8,128)(2,1)} %bitcast.19, ...), custom_call_target="tpu_custom_call" | custom-call | flops 16000000000 | bytes 14000000 | tf_op jit(solution)/shard_map/expert_grad/pallas_call | solution.py:321
  189.5 1.8 copy.10

commit v2 on v1

v2 whole, which is shorter than its diff:
```python
import jax
import jax.numpy as jnp
from jax import lax
from jax.experimental import pallas as pl
from jax.experimental.pallas import tpu as pltpu
from jax.sharding import PartitionSpec as P

MESH = pl.DeviceIdType.MESH
BF = jnp.bfloat16
F32 = jnp.float32
NX, NZ, NY = 4, 8, 4
TOK, W, FFL, CAP = 128, 1792, 256, 40
PAIR = 2 * CAP
CH = NX * PAIR
SLOTS = NX * NZ * CAP
PAIRS = ((0, 1), (-1, 2), (-2, 3), (-3, 4))
WHERE = {j: (c, h) for c, pair in enumerate(PAIRS) for h, j in enumerate(pair)}
NT = W // 256
WIRE = BF
POS = {1: 0, 3: 1, 0: 2, 2: 3}
GROUPS = ((1, 3), (0, 2))
HC = CH // 2
HALF = TOK // 2
PLAN = (
    ("ag", 1, 1), ("ag", 1, 0), ("ag", 2, 1), ("select", 0), ("send", 0, 1), ("ag", 2, 0), ("prepare",),
    ("ag", 3, 1), ("first", 0, 1), ("select", 1), ("send", 1, 1), ("send", 1, 0), ("ag", 3, 0), ("grads", 0, 1),
    ("ag", 4, 1), ("first", 1, 1), ("select", 2), ("ag", 4, 0), ("forward", 0, 1), ("send", 2, 0), ("grads", 1, 1),
    ("select", 3), ("first", 1, 0), ("send", 3, 1), ("send", 3, 0), ("first", 2, 0), ("send", 0, 0),
    ("second", 0, 1), ("forward", 1, 1), ("first", 3, 1), ("send", 2, 1), ("grads", 2, 0), ("grads", 3, 1),
    ("second", 1, 1), ("first", 3, 0), ("forward", 2, 0), ("give", 1, 1), ("forward", 3, 1), ("grads", 3, 0),
    ("first", 2, 1), ("second", 2, 0), ("give", 2, 0), ("second", 3, 1), ("give", 3, 1), ("forward", 3, 0),
    ("grads", 2, 1), ("second", 3, 0), ("forward", 2, 1), ("grads", 1, 0), ("first", 0, 0), ("give", 3, 0),
    ("second", 2, 1), ("forward", 1, 0), ("give", 2, 1), ("combine", 3), ("chain", 1, 4, 0), ("chain", -1, 4, 1),
    ("grads", 0, 0), ("second", 1, 0), ("give", 1, 0), ("chain", -1, 3, 0), ("combine", 2), ("chain", 1, 3, 1),
    ("forward", 0, 0), ("chain", -1, 3, 1), ("give", 0, 1), ("chain", 1, 3, 0), ("combine", 1), ("chain", -1, 2, 0),
    ("chain", 1, 2, 1), ("second", 0, 0), ("give", 0, 0), ("chain", -1, 2, 1), ("chain", 1, 2, 0), ("combine", 0),
    ("chain", -1, 1, 0), ("chain", 1, 1, 1), ("chain", -1, 1, 1), ("chain", 1, 1, 0), ("finish",),
)


def kernel(tokens, meta, wg, wu, wd, gsv, usv, out,
           tok, mt, sel, ghi, glo, xs, rows, hacc, part, hrecv, gu, ret, C, inp, inm, fin,
           gT, uT, gv, uv, wgv, wuv, wdv,
           ag_s, ag_r, rs_s, rs_r, m_s, m_r, xd_s, xd_r, xr_s, xr_r, yr_s, yr_r, yg_s, yg_r, f_s, f_r, loc):
    s = lax.axis_index("section")
    e = lax.axis_index("ep")
    y = lax.axis_index("tp")
    x = e // NZ
    z = lax.rem(e, NZ)

    def zdev(d):
        return (s, x * NZ + lax.rem(z + d + NZ, NZ), y)

    def xdev(o):
        return (s, lax.rem(x + o, NX) * NZ + z, y)

    def ydev(o):
        return (s, e, lax.rem(y + o, NY))

    partner = (1 - s, e, y)

    def remote(src, dst, ss, rs, dev):
        return pltpu.make_async_remote_copy(
            src_ref=src, dst_ref=dst, send_sem=ss, recv_sem=rs, device_id=dev, device_id_type=MESH)

    own_tok = pltpu.make_async_copy(tokens, tok.at[0, pl.ds(0, TOK)], loc.at[0])
    own_meta = pltpu.make_async_copy(meta, mt.at[0], loc.at[1])
    gcopy = pltpu.make_async_copy(gsv, gv, loc.at[2])
    ucopy = pltpu.make_async_copy(usv, uv, loc.at[3])
    dcopy = pltpu.make_async_copy(wd, wdv, loc.at[4])
    wgcopy = pltpu.make_async_copy(wg, wgv, loc.at[5])
    wucopy = pltpu.make_async_copy(wu, wuv, loc.at[6])
    locals_left = dict(tok=own_tok, meta=own_meta, gs=gcopy, us=ucopy, down=dcopy, wgate=wgcopy, wup=wucopy)
    for c in locals_left.values():
        c.start()

    def local(*names):
        for n in names:
            if n in locals_left:
                locals_left.pop(n).wait()

    barrier = pltpu.get_barrier_semaphore()
    peers = [zdev(1), zdev(-1)] + [xdev(o) for o in (1, 2, 3)] + [ydev(o) for o in (1, 2, 3)] + [partner]
    for dev in peers:
        pl.semaphore_signal(barrier, inc=1, device_id=dev, device_id_type=MESH)
    pl.semaphore_wait(barrier, len(peers))

    sends, pending, begun = {}, {}, set()

    def begin(key, copy, landing=None):
        copy.start()
        begun.add(key)
        sends[key] = copy
        pending[key] = landing or copy

    def arrived(key):
        if key in pending:
            pending.pop(key).wait_recv()

    def left(key):
        if key in sends:
            sends.pop(key).wait_send()

    def block(j, lo=0, n=TOK):
        c, h = WHERE[j]
        return tok.at[c, pl.ds(h * TOK + lo, n)]

    def metaof(j):
        c, h = WHERE[j]
        return mt.at[2 * c + h]

    def side(sign):
        return (1 - sign) // 2

    def ag(d, h):
        k = d - 1
        if d == 1:
            local("tok", "meta")
        for sign in ((1, -1) if d < 4 else ((1,), (-1,))[h]):
            i = side(sign)
            arrived(("a", k, sign, h))
            begin(("a", d, sign, h), remote(block(sign * k, h * HALF, HALF), block(d if d == 4 else sign * d, h * HALF, HALF),
                                            ag_s.at[i, k, h], ag_r.at[i, k, h], zdev(-sign)))
            if h == 0:
                arrived(("m", k, sign))
                begin(("m", d, sign), remote(metaof(sign * k), metaof(d if d == 4 else sign * d),
                                             m_s.at[i, k], m_r.at[i, k], zdev(-sign)))

    def columns(n):
        return pl.ds(pl.multiple_of(n * 256, 256), 256)

    def select(c):
        for j in PAIRS[c]:
            for sign in (1, -1) if j == 4 else (1,) if j > 0 else (-1,):
                arrived(("m", abs(j), sign))
                for h in range(2):
                    arrived(("a", abs(j), sign, h))
        t0 = lax.broadcasted_iota(jnp.int32, (TOK, TOK), 0)
        t1 = lax.broadcasted_iota(jnp.int32, (TOK, TOK), 1)
        earlier = (t0 < t1).astype(F32).astype(BF)
        rr = lax.broadcasted_iota(jnp.int32, (PAIR, 2 * TOK), 0)
        cc = lax.broadcasted_iota(jnp.int32, (PAIR, 2 * TOK), 1)
        same = (rr >= CAP) == (cc >= TOK)
        slot = jnp.where(rr >= CAP, rr - CAP, rr).astype(F32)
        r8 = lax.broadcasted_iota(jnp.int32, (8, TOK), 0)
        named, place, gate = [], [], []
        for h in range(2):
            ids = mt[2 * c + h, 0:8, :]
            gts = mt[2 * c + h, 8:16, :]
            m8 = jnp.zeros((8, TOK), F32)
            gs = []
            for o in range(NX):
                want = (lax.rem(x + o, NX) * NZ + z).astype(F32)
                hit = ids == want
                m = jnp.sum(hit.astype(F32), axis=0, keepdims=True)
                gs.append(jnp.sum(jnp.where(hit, gts, 0.0), axis=0, keepdims=True))
                m8 = jnp.where(r8 == o, m, m8)
            pos = jnp.dot(m8.astype(BF), earlier, preferred_element_type=F32)
            pos = jnp.where(m8 > 0.5, pos, -1.0)
            place.append(pos)
            gate.append(gs)
        for o in range(NX):
            pos2 = jnp.concatenate([place[0][o:o + 1], place[1][o:o + 1]], axis=1)
            g2 = jnp.concatenate([gate[0][o], gate[1][o]], axis=1)
            g_hi = g2.astype(BF).astype(F32)
            g_lo = g2 - g_hi
            hit = jnp.logical_and(slot == pos2, same)
            at = pl.ds(POS[o] * PAIR, PAIR)
            sel[c, at, :] = jnp.where(hit, 1.0, 0.0).astype(BF)
            ghi[c, at, :] = jnp.where(hit, g_hi, 0.0).astype(BF)
            glo[c, at, :] = jnp.where(hit, g_lo, 0.0).astype(BF)

        @pl.loop(0, NT, unroll=True)
        def _(n):
            got = jnp.dot(sel[c], tok[c, :, columns(n)], preferred_element_type=F32).astype(BF)
            xs[c, pl.ds(0, HC), columns(n)] = got[0:HC]
            rows[c, pl.ds(HC, PAIR), columns(n)] = got[HC:HC + PAIR]
            xs[c, pl.ds(HC + PAIR, PAIR), columns(n)] = got[HC + PAIR:]

    def across(name, c, g, dst, ss, rs):
        for o in GROUPS[g]:
            if o:
                begin((name, c, o), remote(xs.at[c, pl.ds(POS[o] * PAIR, PAIR)], dst.at[c, pl.ds(POS[NX - o] * PAIR, PAIR)],
                                           ss.at[c, o - 1], rs.at[c, o - 1], xdev(o)))

    def send(c, g):
        across("xd", c, g, rows, xd_s, xd_r)

    def give(c, g):
        across("xr", c, g, ret, xr_s, xr_r)

    def first(c, g):
        local("down")
        for o in GROUPS[g]:
            arrived(("xd", c, o))
        part_rows = pl.ds(g * HC, HC)
        for o in (2, 1, 3, 0):
            q = lax.rem(y + o, NY)
            acc = lax.dot_general(rows[c, part_rows, :], wdv[columns(q), :], (((1,), (1,)), ((), ())), preferred_element_type=F32)
            if o:
                part[c, g, o - 1] = acc.astype(WIRE)
                begin(("yr", c, g, o), remote(part.at[c, g, o - 1], hrecv.at[c, g, o - 1],
                                              yr_s.at[c, g, o - 1], yr_r.at[c, g, o - 1], ydev(o)))
            else:
                hacc[c, part_rows, :] = acc

    def grads(c, g):
        for o in (1, 2, 3):
            arrived(("yr", c, g, o))
        j1, j2 = PAIRS[c]
        for i, o in enumerate(GROUPS[g]):
            at = pl.ds(i * PAIR, PAIR)
            h = hacc[c, pl.ds(POS[o] * PAIR, PAIR), :]
            for k in range(3):
                h = h + hrecv[c, g, k, at, :].astype(F32)
            base = lax.rem(x + o, NX) * NZ
            b1 = pl.ds(pl.multiple_of((base + lax.rem(z + j1 + NZ, NZ)) * CAP, 8), CAP)
            b2 = pl.ds(pl.multiple_of((base + lax.rem(z + j2 + NZ, NZ)) * CAP, 8), CAP)
            a = jnp.concatenate([gT[b1, :], gT[b2, :]], axis=0)
            u = jnp.concatenate([uT[b1, :], uT[b2, :]], axis=0)
            sigma = 1.0 / (1.0 + jnp.exp(-a))
            gu[c, y, g, 0, at, :] = (h * u * sigma * (1.0 + a * (1.0 - sigma))).astype(BF)
            gu[c, y, g, 1, at, :] = (h * a * sigma).astype(BF)
        for k, step in enumerate((1, NY - 1)):
            swap(c, g, k, step, y, slice(None))

    def swap(c, g, k, step, holder, what):
        src = gu.at[c, holder, g] if what == slice(None) else gu.at[c, holder, g, what]
        origin = lax.rem(holder + NY - step, NY)
        landing = gu.at[c, origin, g] if what == slice(None) else gu.at[c, origin, g, what]
        ss, rs = yg_s.at[c, g, k], yg_r.at[c, g, k]
        begin(("yg", c, g, k), remote(src, src, ss, rs, ydev(step)), remote(landing, landing, ss, rs, ydev(step)))

    def forward(c, g):
        for k in range(2):
            arrived(("yg", c, g, k))
        for k, step in enumerate((1, NY - 1)):
            swap(c, g, 2 + k, step, lax.rem(y + NY - step, NY), k)

    def second(c, g):
        local("wgate", "wup")
        for o in GROUPS[g]:
            left(("xd", c, o))
        for k in range(4):
            arrived(("yg", c, g, k))

        @pl.loop(0, NT, unroll=True)
        def _(n):
            acc = jnp.zeros((HC, 256), F32)
            for q in range(NY):
                for i, w in ((0, wgv), (1, wuv)):
                    acc = acc + lax.dot_general(gu[c, q, g, i], w[columns(n), q * 256:(q + 1) * 256], (((1,), (1,)), ((), ())), preferred_element_type=F32)
            acc = acc.astype(BF)
            if g == 0:
                xs[c, pl.ds(0, HC), columns(n)] = acc
            else:
                ret[c, pl.ds(HC, PAIR), columns(n)] = acc[0:PAIR]
                xs[c, pl.ds(HC + PAIR, PAIR), columns(n)] = acc[PAIR:]

    def combine(c):
        for o in (1, 3, 2):
            arrived(("xr", c, o))

        @pl.loop(0, NT, unroll=True)
        def _(n):
            r = ret[c, :, columns(n)]
            dims = (((0,), (0,)), ((), ()))
            C[c, :, columns(n)] = (lax.dot_general(ghi[c], r, dims, preferred_element_type=F32)
                                   + lax.dot_general(glo[c], r, dims, preferred_element_type=F32))

    def csum(j, lo, n, extra):
        c, h = WHERE[j]
        base = h * TOK + lo
        value = C[c, pl.ds(base, n), :]
        for r in extra:
            value = value + r.astype(F32)
        return value

    def chain(sign, j, h):
        for key in list(sends):
            if key[0] == "a":
                left(key)
        inbox = inp if sign > 0 else inm
        i, lo = side(sign), h * HALF
        arrived(("r", sign, j + 1, h))
        extra = (inbox[j, pl.ds(lo, HALF), :],) if ("r", sign, j + 1, h) in begun else ()
        at = 4 if j == 4 else sign * j
        block(at, lo, HALF)[...] = csum(at, lo, HALF, extra).astype(BF)
        begin(("r", sign, j, h), remote(block(at, lo, HALF), inbox.at[j - 1, pl.ds(lo, HALF)],
                                        rs_s.at[i, j - 1, h], rs_r.at[i, j - 1, h], zdev(sign)))

    def prepare():
        local("gs", "us")

        @pl.loop(0, SLOTS // 256)
        def _(i):
            gT[columns(i), :] = gv[:, columns(i)].astype(F32).T
            uT[columns(i), :] = uv[:, columns(i)].astype(F32).T

    def finish():
        for h in range(2):
            for sign in (1, -1):
                arrived(("r", sign, 1, h))
            at = pl.ds(h * HALF, HALF)
            fin[at, :] = csum(0, h * HALF, HALF, (inp[0, at, :], inm[0, at, :])).astype(BF)
        begin(("f",), remote(fin, out, f_s, f_r, partner))
        arrived(("f",))

    verbs = dict(ag=ag, prepare=prepare, select=select, send=send, first=first, grads=grads, second=second, give=give,
                 forward=forward, combine=combine, chain=chain, finish=finish)
    for verb, *args in PLAN:
        verbs[verb](*args)
    for key in list(pending):
        arrived(key)
    for key in list(sends):
        left(key)


def shards(out_grad, expert_ids, gates, w_gate, w_up, w_down, gate_saved, up_saved):
    meta = jnp.concatenate([expert_ids[0].T.astype(F32), gates[0].T], axis=0)
    dma = pltpu.SemaphoreType.DMA
    done = pl.pallas_call(
        kernel,
        out_shape=jax.ShapeDtypeStruct((TOK, W), BF),
        in_specs=[pl.BlockSpec(memory_space=pl.ANY)] * 7,
        out_specs=pl.BlockSpec(memory_space=pl.ANY),
        scratch_shapes=[
            pltpu.VMEM((4, 2 * TOK, W), BF),
            pltpu.VMEM((8, 16, TOK), F32),
            pltpu.VMEM((4, CH, 2 * TOK), BF),
            pltpu.VMEM((4, CH, 2 * TOK), BF),
            pltpu.VMEM((4, CH, 2 * TOK), BF),
            pltpu.VMEM((4, CH, W), BF),
            pltpu.VMEM((4, CH, W), BF),
            pltpu.VMEM((4, CH, FFL), F32),
            pltpu.VMEM((4, 2, 3, HC, FFL), WIRE),
            pltpu.VMEM((4, 2, 3, HC, FFL), WIRE),
            pltpu.VMEM((4, NY, 2, 2, HC, FFL), BF),
            pltpu.VMEM((4, CH, W), BF),
            pltpu.VMEM((4, 2 * TOK, W), F32),
            pltpu.VMEM((4, TOK, W), BF),
            pltpu.VMEM((4, TOK, W), BF),
            pltpu.VMEM((TOK, W), BF),
            pltpu.VMEM((SLOTS, FFL), F32),
            pltpu.VMEM((SLOTS, FFL), F32),
            pltpu.VMEM((FFL, SLOTS), BF),
            pltpu.VMEM((FFL, SLOTS), BF),
            pltpu.VMEM((W, 1024), BF),
            pltpu.VMEM((W, 1024), BF),
            pltpu.VMEM((1024, W), BF),
        ] + [dma((2, 4, 2))] * 4 + [dma((2, 4))] * 2 + [dma((4, 3))] * 4 + [dma((4, 2, 3))] * 2 + [dma((4, 2, 4))] * 2 + [dma, dma, dma((7,))],
        compiler_params=pltpu.CompilerParams(
            collective_id=0, has_side_effects=True, vmem_limit_bytes=63 * 2**20),
        cost_estimate=pl.CostEstimate(flops=16 * 10**9, bytes_accessed=14 * 10**6, transcendentals=3 * 10**5),
        name="expert_grad",
    )(out_grad[0], meta, w_gate[0, 0], w_up[0, 0], w_down[0, 0], gate_saved[0, 0], up_saved[0, 0])
    return done[None]


def solution(mesh):
    return jax.shard_map(
        shards,
        mesh=mesh,
        in_specs=(
            P("section", "ep", "tp"),
            P("section", "ep", None),
            P("section", "ep", None),
            P("section", "ep", "tp", None),
            P("section", "ep", "tp", None),
            P("section", "ep", None, "tp"),
            P("section", "ep", "tp", None),
            P("section", "ep", "tp", None),
        ),
        out_specs=P("section", "ep", "tp"),
        check_vma=False,
    )
```

time: 193 us -> 153 us (0.79)
  Pallas kernels: 187 us -> 149 us
    pallas_call x1, Pallas kernels: 187 us -> 149 us  [shards(): pl.pallas_call(kernel, out_shape=jax.ShapeDtypeStruct((TOK, W), BF), in_s...]
where the time goes in v2:
time: 153 us
  Pallas kernels  149 us (97%)
  other arithmetic  1.97 us (1%)
  local copies, waits for them, and re-layouts  1.82 us (1%)
    pallas_call x1, Pallas kernels, shards(): pl.pallas_call(kernel, out_shape=jax.ShapeDtypeStruct((TOK, W), BF), in_s...  149 us

profile of v2, /device:TPU:1, one launch (start us, length us, event | category | flops | bytes accessed | tf_op | source)
XLA Modules:
  0.0 153.2 jit_solution(14064148355474136874)
XLA Ops:
  0.0 0.7 convert_bitcast_fusion
  0.7 1.3 pad_maximum_fusion.meta
  2.0 149.4 %expert_grad.1 = bf16[128,1792]{1,0:T(8,128)(2,1)} custom-call(bf16[128,1792]{1,0:T(8,128)(2,1)} %bitcast.21, f32[16,128]{1,0:T(8,128)} %pad_maximum_fusion.meta, bf16[1792,1024]{1,0:T(8,128)(2,1)} %bitcast.16, bf16[1792,1024]{1,0:T(8,128)(2,1)} %bitcast.17, bf16[1024,1792]{1,0:T(8,128)(2,1)} %bitcast.18, bf16[256,1280]{1,0:T(8,128)(2,1)} %bitcast.19, ...), custom_call_target="tpu_custom_call" | custom-call | flops 16000000000 | bytes 14000000 | tf_op jit(solution)/shard_map/expert_grad/pallas_call | solution.py:322
  151.4 1.8 %copy.10 = bf16[1,128,1792]{2,1,0:T(8,128)(2,1)} copy(bf16[1,128,1792]{2,1,0:T(8,128)(2,1)} %bitcast.14) | data formatting | bytes 917504

commit v3 on v2

--- a/solution.py
+++ b/solution.py
@@ -38,9 +38,9 @@
 )
 
 
-def kernel(tokens, meta, wg, wu, wd, gsv, usv, out,
+def kernel(tokens, ids_in, gates_in, wg, wu, wd, gsv, usv, out,
            tok, mt, sel, ghi, glo, xs, rows, hacc, part, hrecv, gu, ret, C, inp, inm, fin,
-           gT, uT, gv, uv, wgv, wuv, wdv,
+           gT, uT, gv, uv, wgv, wuv, wdv, idv, gtv,
            ag_s, ag_r, rs_s, rs_r, m_s, m_r, xd_s, xd_r, xr_s, xr_r, yr_s, yr_r, yg_s, yg_r, f_s, f_r, loc):
     s = lax.axis_index("section")
     e = lax.axis_index("ep")
@@ -64,13 +64,14 @@
             src_ref=src, dst_ref=dst, send_sem=ss, recv_sem=rs, device_id=dev, device_id_type=MESH)
 
     own_tok = pltpu.make_async_copy(tokens, tok.at[0, pl.ds(0, TOK)], loc.at[0])
-    own_meta = pltpu.make_async_copy(meta, mt.at[0], loc.at[1])
+    own_ids = pltpu.make_async_copy(ids_in, idv, loc.at[1])
+    own_gates = pltpu.make_async_copy(gates_in, gtv, loc.at[7])
     gcopy = pltpu.make_async_copy(gsv, gv, loc.at[2])
     ucopy = pltpu.make_async_copy(usv, uv, loc.at[3])
     dcopy = pltpu.make_async_copy(wd, wdv, loc.at[4])
     wgcopy = pltpu.make_async_copy(wg, wgv, loc.at[5])
     wucopy = pltpu.make_async_copy(wu, wuv, loc.at[6])
-    locals_left = dict(tok=own_tok, meta=own_meta, gs=gcopy, us=ucopy, down=dcopy, wgate=wgcopy, wup=wucopy)
+    locals_left = dict(tok=own_tok, ids=own_ids, gates=own_gates, gs=gcopy, us=ucopy, down=dcopy, wgate=wgcopy, wup=wucopy)
     for c in locals_left.values():
         c.start()
 
@@ -83,6 +84,9 @@
     peers = [zdev(1), zdev(-1)] + [xdev(o) for o in (1, 2, 3)] + [ydev(o) for o in (1, 2, 3)] + [partner]
     for dev in peers:
         pl.semaphore_signal(barrier, inc=1, device_id=dev, device_id_type=MESH)
+    local("ids", "gates")
+    mt[0, 0:8, :] = idv[...].astype(F32)
+    mt[0, 8:16, :] = gtv[...]
     pl.semaphore_wait(barrier, len(peers))
 
     sends, pending, begun = {}, {}, set()
@@ -115,7 +119,7 @@
     def ag(d, h):
         k = d - 1
         if d == 1:
-            local("tok", "meta")
+            local("tok")
         for sign in ((1, -1) if d < 4 else ((1,), (-1,))[h]):
             i = side(sign)
             arrived(("a", k, sign, h))
@@ -317,12 +321,11 @@
 
 
 def shards(out_grad, expert_ids, gates, w_gate, w_up, w_down, gate_saved, up_saved):
-    meta = jnp.concatenate([expert_ids[0].T.astype(F32), gates[0].T], axis=0)
     dma = pltpu.SemaphoreType.DMA
     done = pl.pallas_call(
         kernel,
         out_shape=jax.ShapeDtypeStruct((TOK, W), BF),
-        in_specs=[pl.BlockSpec(memory_space=pl.ANY)] * 7,
+        in_specs=[pl.BlockSpec(memory_space=pl.ANY)] * 8,
         out_specs=pl.BlockSpec(memory_space=pl.ANY),
         scratch_shapes=[
             pltpu.VMEM((4, 2 * TOK, W), BF),
@@ -348,12 +351,14 @@
             pltpu.VMEM((W, 1024), BF),
             pltpu.VMEM((W, 1024), BF),
             pltpu.VMEM((1024, W), BF),
-        ] + [dma((2, 4, 2))] * 4 + [dma((2, 4))] * 2 + [dma((4, 3))] * 4 + [dma((4, 2, 3))] * 2 + [dma((4, 2, 4))] * 2 + [dma, dma, dma((7,))],
+            pltpu.VMEM((8, TOK), jnp.int32),
+            pltpu.VMEM((8, TOK), F32),
+        ] + [dma((2, 4, 2))] * 4 + [dma((2, 4))] * 2 + [dma((4, 3))] * 4 + [dma((4, 2, 3))] * 2 + [dma((4, 2, 4))] * 2 + [dma, dma, dma((8,))],
         compiler_params=pltpu.CompilerParams(
             collective_id=0, has_side_effects=True, vmem_limit_bytes=63 * 2**20),
         cost_estimate=pl.CostEstimate(flops=16 * 10**9, bytes_accessed=14 * 10**6, transcendentals=3 * 10**5),
         name="expert_grad",
-    )(out_grad[0], meta, w_gate[0, 0], w_up[0, 0], w_down[0, 0], gate_saved[0, 0], up_saved[0, 0])
+    )(out_grad[0], expert_ids[0].T, gates[0].T, w_gate[0, 0], w_up[0, 0], w_down[0, 0], gate_saved[0, 0], up_saved[0, 0])
     return done[None]
 
 

time: 153 us -> 151 us (0.987)
  other arithmetic: 1.97 us -> 0 us
where the time goes in v3:
time: 151 us
  Pallas kernels  150 us (99%)
  local copies, waits for them, and re-layouts  1.82 us (1%)
    pallas_call x1, Pallas kernels, shards(): pl.pallas_call(kernel, out_shape=jax.ShapeDtypeStruct((TOK, W), BF), in_s...  150 us

profile of v3, /device:TPU:1, one launch (start us, length us, event | category | flops | bytes accessed | tf_op | source)
XLA Modules:
  0.0 151.4 jit_solution(9789559483568019931)
XLA Ops:
  0.0 149.5 %expert_grad.1 = bf16[128,1792]{1,0:T(8,128)(2,1)} custom-call(bf16[128,1792]{1,0:T(8,128)(2,1)} %bitcast.19, s32[8,128]{1,0:T(8,128)} %bitcast.20, f32[8,128]{1,0:T(8,128)} %bitcast.21, bf16[1792,1024]{1,0:T(8,128)(2,1)} %bitcast.14, bf16[1792,1024]{1,0:T(8,128)(2,1)} %bitcast.15, bf16[1024,1792]{1,0:T(8,128)(2,1)} %bitcast.16, bf16[256,1280]{1,0:T(8,128)(2,1)} %bitcast.17, ...), custom_call_target="tpu_custom_call" | custom-call | flops 16000000000 | bytes 14000000 | tf_op jit(solution)/shard_map/expert_grad/pallas_call | solution.py:325
  149.6 1.8 %copy.10 = bf16[1,128,1792]{2,1,0:T(8,128)(2,1)} copy(bf16[1,128,1792]{2,1,0:T(8,128)(2,1)} %bitcast.13) | data formatting | bytes 917504

commit v4 on v3

--- a/solution.py
+++ b/solution.py
@@ -22,19 +22,19 @@
 HC = CH // 2
 HALF = TOK // 2
 PLAN = (
-    ("ag", 1, 1), ("ag", 1, 0), ("ag", 2, 1), ("select", 0), ("send", 0, 1), ("ag", 2, 0), ("prepare",),
-    ("ag", 3, 1), ("first", 0, 1), ("select", 1), ("send", 1, 1), ("send", 1, 0), ("ag", 3, 0), ("grads", 0, 1),
-    ("ag", 4, 1), ("first", 1, 1), ("select", 2), ("ag", 4, 0), ("forward", 0, 1), ("send", 2, 0), ("grads", 1, 1),
-    ("select", 3), ("first", 1, 0), ("send", 3, 1), ("send", 3, 0), ("first", 2, 0), ("send", 0, 0),
-    ("second", 0, 1), ("forward", 1, 1), ("first", 3, 1), ("send", 2, 1), ("grads", 2, 0), ("grads", 3, 1),
-    ("second", 1, 1), ("first", 3, 0), ("forward", 2, 0), ("give", 1, 1), ("forward", 3, 1), ("grads", 3, 0),
-    ("first", 2, 1), ("second", 2, 0), ("give", 2, 0), ("second", 3, 1), ("give", 3, 1), ("forward", 3, 0),
-    ("grads", 2, 1), ("second", 3, 0), ("forward", 2, 1), ("grads", 1, 0), ("first", 0, 0), ("give", 3, 0),
-    ("second", 2, 1), ("forward", 1, 0), ("give", 2, 1), ("combine", 3), ("chain", 1, 4, 0), ("chain", -1, 4, 1),
-    ("grads", 0, 0), ("second", 1, 0), ("give", 1, 0), ("chain", -1, 3, 0), ("combine", 2), ("chain", 1, 3, 1),
-    ("forward", 0, 0), ("chain", -1, 3, 1), ("give", 0, 1), ("chain", 1, 3, 0), ("combine", 1), ("chain", -1, 2, 0),
-    ("chain", 1, 2, 1), ("second", 0, 0), ("give", 0, 0), ("chain", -1, 2, 1), ("chain", 1, 2, 0), ("combine", 0),
-    ("chain", -1, 1, 0), ("chain", 1, 1, 1), ("chain", -1, 1, 1), ("chain", 1, 1, 0), ("finish",),
+    ("ag", 1, 0), ("prepare",), ("ag", 1, 1), ("ag", 2, 0), ("select", 0), ("send", 0, 0), ("ag", 2, 1),
+    ("ag", 3, 0), ("select", 1), ("send", 1, 0), ("ag", 3, 1), ("first", 0, 0), ("send", 1, 1), ("grads", 0, 0),
+    ("first", 1, 0), ("ag", 4, 0), ("ag", 4, 1), ("select", 2), ("send", 2, 0), ("first", 1, 1), ("select", 3),
+    ("send", 3, 0), ("grads", 1, 0), ("first", 2, 0), ("send", 2, 1), ("forward", 1, 0), ("first", 3, 0),
+    ("grads", 2, 0), ("send", 3, 1), ("second", 1, 0), ("grads", 3, 0), ("send", 0, 1), ("forward", 2, 0),
+    ("give", 1, 0), ("first", 3, 1), ("forward", 3, 0), ("first", 2, 1), ("second", 2, 0), ("grads", 3, 1),
+    ("second", 3, 0), ("give", 2, 0), ("grads", 2, 1), ("give", 3, 0), ("forward", 3, 1), ("grads", 1, 1),
+    ("forward", 2, 1), ("first", 0, 1), ("second", 3, 1), ("give", 3, 1), ("forward", 1, 1), ("second", 2, 1),
+    ("give", 2, 1), ("grads", 0, 1), ("combine", 3), ("forward", 0, 0), ("chain", 1, 4, 0), ("chain", -1, 4, 1),
+    ("second", 1, 1), ("forward", 0, 1), ("give", 1, 1), ("chain", -1, 3, 0), ("combine", 2), ("chain", 1, 3, 1),
+    ("second", 0, 0), ("give", 0, 0), ("chain", 1, 3, 0), ("chain", -1, 3, 1), ("second", 0, 1), ("give", 0, 1),
+    ("chain", -1, 2, 0), ("combine", 1), ("chain", 1, 2, 1), ("chain", 1, 2, 0), ("chain", -1, 2, 1),
+    ("chain", -1, 1, 0), ("combine", 0), ("chain", 1, 1, 1), ("chain", 1, 1, 0), ("chain", -1, 1, 1), ("finish",),
 )
 
 

time: 151 us -> 156 us (1.033); the launches traced: 151 us -> 155 us
  Pallas kernels: 150 us -> 153 us
    pallas_call x1, Pallas kernels: 150 us -> 153 us  [shards(): pl.pallas_call(kernel, out_shape=jax.ShapeDtypeStruct((TOK, W), BF), in_s...]
where the time goes in v4:
time: 156 us; the launch traced here: 155 us
  Pallas kernels  153 us (98%)
  local copies, waits for them, and re-layouts  1.82 us (1%)
    pallas_call x1, Pallas kernels, shards(): pl.pallas_call(kernel, out_shape=jax.ShapeDtypeStruct((TOK, W), BF), in_s...  153 us

profile of v4, /device:TPU:1, one launch (start us, length us, event | category | flops | bytes accessed | tf_op | source)
XLA Modules:
  0.0 154.8 jit_solution(6200807167795221219)
XLA Ops:
  0.0 153.0 %expert_grad.1 = bf16[128,1792]{1,0:T(8,128)(2,1)} custom-call(bf16[128,1792]{1,0:T(8,128)(2,1)} %bitcast.19, s32[8,128]{1,0:T(8,128)} %bitcast.20, f32[8,128]{1,0:T(8,128)} %bitcast.21, bf16[1792,1024]{1,0:T(8,128)(2,1)} %bitcast.14, bf16[1792,1024]{1,0:T(8,128)(2,1)} %bitcast.15, bf16[1024,1792]{1,0:T(8,128)(2,1)} %bitcast.16, bf16[256,1280]{1,0:T(8,128)(2,1)} %bitcast.17, ...), custom_call_target="tpu_custom_call" | custom-call | flops 16000000000 | bytes 14000000 | tf_op jit(solution)/shard_map/expert_grad/pallas_call | solution.py:325
  153.0 1.8 %copy.10 = bf16[1,128,1792]{2,1,0:T(8,128)(2,1)} copy(bf16[1,128,1792]{2,1,0:T(8,128)(2,1)} %bitcast.13) | data formatting | bytes 917504
